TPU v7x, 32 devices: a whole 2x2x4 slice. The times are simulated.
32 devices in a mesh: rollout: 16 (over z, y, core), tensor: 2 (over x).
Axes of the slice: x: 2, y: 2, z: 4, core: 2. Of those that a mesh axis runs over, the one named last changes fastest.
Arguments:
- tokens: bfloat16 [4096, 8192], P('rollout', 'tensor'), may hold values from -6 to 6
- base_key_value_weight: bfloat16 [8192, 2, 1024], P(None, None, 'tensor'), may hold values from -0.0625 to 0.0625
- key_value_bias: bfloat16 [2, 1024], P(None, 'tensor'), may hold values from -3 to 3
- adapter_down_blocks: bfloat16 [8192, 2, 128], P('rollout'), may hold values from -0.0625 to 0.0625
- adapter_up_blocks: bfloat16 [2, 128, 1024], P(None, 'rollout', 'tensor'), may hold values from -0.29882812 to 0.29882812
- owner_shard_lookup: int32 [16], replicated, may hold values from 0 to 15, each once
- lengths: int32 [16, 8], P('rollout'), may hold values from 1 to 128, 256 in all within a row
- routes: int32 [4096], P('rollout'), may hold values from 0 to 15, as said below
Outputs:
- kv_cache: bfloat16 [8192, 2, 1024], P('rollout', None, 'tensor')
Inputs may be any that keep to these rules, and one draw needn't show every extreme that they name: `owner_shard_lookup`: a permutation of the rollout indices. `routes`: the rows of one group name each destination at most 32 times; one destination, drawn from the seed, is named exactly 32 times by every group.
All inputs are finite; a program needn't handle non-finite values.
Results may differ from a plain program's by a relative error of at most 0.0048.
Values may be sent and summed in bfloat16 or wider, within the bound.
A program may use at most 128 MiB of HBM per device.

v0:
```python
import jax
import jax.numpy as jnp
from jax import lax
from jax.sharding import PartitionSpec as P

HEAD = 128


adapter_scale = 2.0
rope_base = 1000000.0


def positions_of(lengths_row, row_count):
    ends = jnp.cumsum(lengths_row)
    starts = ends - lengths_row
    index = jnp.arange(row_count, dtype=jnp.int32)
    begins = jnp.max(jnp.where(starts[None, :] <= index[:, None], starts[None, :], 0), axis=1)
    return index - begins


def rotate(keys, places):
    half_width = HEAD // 2
    frequency = rope_base ** (-(jnp.arange(half_width, dtype=jnp.float32) * 2.0) / HEAD)
    angles = places.astype(jnp.float32)[:, None] * frequency[None, :]
    cosine = jnp.cos(angles)[:, None, :]
    sine = jnp.sin(angles)[:, None, :]
    shaped = keys.reshape(keys.shape[0], -1, HEAD)
    first = shaped[..., :half_width]
    second = shaped[..., half_width:]
    turned = jnp.concatenate(
        [first * cosine - second * sine, second * cosine + first * sine], axis=-1
    )
    return turned.reshape(keys.shape)


def finish_rows(summed, places, key_value_bias):
    width = key_value_bias.shape[1]
    shaped = summed.reshape(summed.shape[0], 2, width) + key_value_bias.astype(jnp.float32)[None]
    keys = rotate(shaped[:, 0], places)
    return jnp.stack([keys, shaped[:, 1]], axis=1)


def slot_index(target, group_count, capacity):
    matches = (target[:, None] == jnp.arange(group_count, dtype=jnp.int32)[None, :]).astype(
        jnp.int32
    )
    order_in = jnp.sum((jnp.cumsum(matches, axis=0) - matches) * matches, axis=1)
    return target * capacity + order_in


def place_rows(send_slots, slot_count, values):
    selector = (jnp.arange(slot_count, dtype=jnp.int32)[:, None] == send_slots[None, :]).astype(
        jnp.bfloat16
    )
    return jnp.dot(selector, values, preferred_element_type=jnp.float32).astype(jnp.bfloat16)


def body(
    tokens,
    base_key_value_weight,
    key_value_bias,
    adapter_down_blocks,
    adapter_up_blocks,
    owner_shard_lookup,
    lengths,
    routes,
):
    group_count = lax.axis_size("rollout")
    own_index = lax.axis_index("rollout")
    row_count = tokens.shape[0]
    capacity = 2 * row_count // group_count
    width = base_key_value_weight.shape[2]
    model_width = base_key_value_weight.shape[0]
    row_block_size = adapter_down_blocks.shape[0]
    inverse_permutation = (
        jnp.zeros((group_count,), jnp.int32)
        .at[owner_shard_lookup]
        .set(jnp.arange(group_count, dtype=jnp.int32))
    )
    up_persisted = lax.all_gather(adapter_up_blocks, "rollout", axis=1, tiled=True)
    rank_block_rows = adapter_up_blocks.shape[1]
    up_gathered = up_persisted.reshape(2, group_count, rank_block_rows, width)[
        :, inverse_permutation
    ].reshape(2, group_count * rank_block_rows, width)
    down_persisted = lax.all_gather(adapter_down_blocks, "rollout", axis=0, tiled=True)
    down_gathered = down_persisted.reshape(group_count, row_block_size, 2, -1)[
        inverse_permutation
    ].reshape(model_width, 2, -1)
    weight_update = jnp.einsum(
        "ohd,hde->ohe", down_gathered, up_gathered, preferred_element_type=jnp.float32
    )
    merged_weight = (
        base_key_value_weight.astype(jnp.float32) + adapter_scale * weight_update
    ).astype(jnp.bfloat16)
    merged_flat = merged_weight.reshape(model_width, 2 * width)
    slot_count = group_count * capacity
    send_slots = slot_index(routes, group_count, capacity)
    all_routes, all_lengths = (
        lax.all_gather(routes, "rollout", axis=0, tiled=True),
        lax.all_gather(lengths, "rollout", axis=0, tiled=True),
    )
    places = jax.vmap(lambda row: positions_of(row, row_count))(all_lengths)
    target = all_routes.reshape(group_count, row_count)
    matches = (target == own_index).astype(jnp.int32)
    order_in = jnp.cumsum(matches, axis=1) - matches
    picked = (matches[:, :, None] == 1) & (
        order_in[:, :, None] == jnp.arange(capacity, dtype=jnp.int32)[None, None, :]
    )
    picked_int = picked.astype(jnp.int32)
    slot_places = jnp.sum(picked_int * places[:, :, None], axis=1).reshape(slot_count)
    live = jnp.sum(picked_int, axis=1).astype(jnp.float32).reshape(slot_count)
    outgoing = place_rows(send_slots, slot_count, tokens)
    outgoing = outgoing.reshape(group_count, capacity, tokens.shape[1])
    arrived = lax.all_to_all(outgoing, "rollout", split_axis=0, concat_axis=0, tiled=True).reshape(
        slot_count, tokens.shape[1]
    )
    summed = jnp.dot(
        lax.all_gather(arrived, "tensor", axis=1, tiled=True),
        merged_flat,
        preferred_element_type=jnp.float32,
    )
    finished = finish_rows(summed, slot_places, key_value_bias) * live[:, None, None]
    return finished.astype(jnp.bfloat16)


def solution(mesh):
    in_specs = (
        P("rollout", "tensor"),
        P(None, None, "tensor"),
        P(None, "tensor"),
        P("rollout", None, None),
        P(None, "rollout", "tensor"),
        P(),
        P("rollout", None),
        P("rollout"),
    )
    out_specs = P("rollout", None, "tensor")
    return jax.shard_map(body, mesh=mesh, in_specs=in_specs, out_specs=out_specs, check_vma=False)
```

profile of v0, /device:TPU:0, one launch (start us, length us, event | category | flops | bytes accessed | tf_op | source)
XLA Modules:
  0.0 286.8 jit_solution(1058796520158536479)
XLA Ops:
  6.5 0.0 copy-start
  6.5 0.8 fusion.19
  7.4 0.6 reduce-window.14
  7.9 0.2 slice_reduce_fusion.1
  8.2 0.8 fusion.18
  8.9 0.7 multiply_add_fusion.1
  9.6 0.0 copy-done
  9.6 3.2 %convolution_convert_fusion = bf16[512,4096]{1,0:T(8,128)(2,1)} fusion(bf16[256,4096]{1,0:T(8,128)(2,1)S(1)} %copy-done, s32[256]{0:T(256)S(1)} %multiply_add_fusion.1), kind=kOutput, calls=%fused_computation.8 | convolution fusion | flops 1075970048 | bytes 6292480 | tf_op jit(solution)/shard_map/dot_general | solution.py:55
  12.8 7.4 %all-to-all-start = ((bf16[16,32,4096]{2,1,0:T(8,128)(2,1)}), bf16[16,32,4096]{2,1,0:T(8,128)(2,1)}, u32[]{:S(2)}, u32[]{:S(2)}) async-start(bf16[16,32,4096]{2,1,0:T(8,128)(2,1)} %bitcast.77), calls=%async_computation | async-start | bytes 8388608 | tf_op jit(solution)/shard_map/all_to_all | solution.py:114
  20.3 0.0 copy-start.4
  20.3 0.0 copy-start.5
  20.3 0.0 copy-start.3
  20.3 0.0 all-gather.7.cloned.1.call-start
  20.3 0.7 all-gather.7.cloned.1.call-update
  21.0 0.0 all-gather.5.cloned.1.call-start
  21.1 102.1 %all-to-all-done = bf16[16,32,4096]{2,1,0:T(8,128)(2,1)} async-done(((bf16[16,32,4096]{2,1,0:T(8,128)(2,1)}), bf16[16,32,4096]{2,1,0:T(8,128)(2,1)}, u32[]{:S(2)}, u32[]{:S(2)}) %all-to-all-start) | async-done | bytes 4194336 | tf_op jit(solution)/shard_map/all_to_all | solution.py:114
  123.2 0.0 all-gather.5.cloned.1.call-update
  123.2 0.0 copy-done.4
  123.3 0.0 copy-done.5
  123.3 35.2 %all-gather.1 = s32[16,1,8]{2,1,0:T(1,128)S(1)} all-gather(s32[1,1,8]{2,1,0:T(1,128)S(1)} %bitcast.86), channel_id=1, replica_groups=mesh['rollout'=16,'tensor'=2] {'rollout'}, dimensions={0}, use_global_device_ids=true | all-gather | bytes 544 | tf_op jit(solution)/shard_map/all_gather | solution.py:100
  158.5 0.1 copy.53
  158.6 0.1 copy.54
  158.7 0.0 copy-done.3
  158.7 17.4 %all-gather = s32[16,1,256]{2,1,0:T(1,128)S(1)} all-gather(s32[1,1,256]{2,1,0:T(1,128)S(1)} %bitcast.85), channel_id=1, replica_groups=mesh['rollout'=16,'tensor'=2] {'rollout'}, dimensions={0}, use_global_device_ids=true | all-gather | bytes 17408 | tf_op jit(solution)/shard_map/all_gather | solution.py:99
  176.1 0.6 reduce-window.16
  176.7 0.2 slice_reduce_fusion
  176.9 0.1 select_reduce_fusion.1
  177.1 0.1 bitcast_subtract_fusion
  177.2 0.6 convert_reduce_fusion
  177.8 0.1 convert_element_type.79
  177.9 0.1 convert_element_type.76
  178.0 41.0 %copy.46 = bf16[8192,2,512]{0,2,1:T(8,128)(2,1)} copy(bf16[8192,2,512]{2,1,0:T(2,128)(2,1)} %param.9) | data formatting | bytes 33554432 | tf_op args[1]
  219.0 0.0 copy-done.6
  219.0 0.6 scatter_custom_fusion
  219.7 0.0 copy-done.2
  219.7 19.5 %all_gather.16 = bf16[2,128,512]{2,1,0:T(8,128)(2,1)S(1)} all-gather(bf16[2,8,512]{2,1,0:T(8,128)(2,1)S(1)} %copy-done.2), channel_id=1, replica_groups=mesh['rollout'=16,'tensor'=2] {'rollout'}, dimensions={1}, use_global_device_ids=true | all-gather | bytes 278528 | tf_op jit(solution)/shard_map/all_gather | solution.py:80
  239.2 0.6 gather_fusion
  239.8 0.5 multiply_cosine_fusion
  240.3 0.0 all-gather.7.cloned.1.call-done
  240.4 12.2 %gather_fusion.1 = bf16[16,512,2,128]{3,2,1,0:T(2,128)(2,1)} fusion(bf16[16,512,2,128]{3,2,1,0:T(2,128)(2,1)} %bitcast.78, s32[1024]{0:T(1024)S(1)} %pad_clamp_fusion), kind=kCustom, calls=%fused_computation.1 | custom fusion | bytes 8388672 | tf_op jit(solution)/shard_map/gather | solution.py:86
  252.5 5.1 %copy.48 = bf16[16,512,2,128]{3,1,0,2:T(8,128)(2,1)} copy(bf16[16,512,2,128]{3,2,1,0:T(2,128)(2,1)} %gather_fusion.1) | data formatting | bytes 8388608 | tf_op jit(solution)/shard_map/gather | solution.py:86
  257.6 19.5 %fusion.5 = f32[512,2,512]{0,2,1:T(8,128)S(1)} fusion(bf16[8192,2,128]{2,0,1:T(8,128)(2,1)} %bitcast.79, bf16[8192,2,512]{0,2,1:T(8,128)(2,1)} %copy.46, bf16[512,8192]{1,0:T(8,128)(2,1)} %all-gather.5.cloned.1.call-done, f32[2,512]{1,0:T(2,128)S(1)} %convert_element_type.70, bf16[16,2,8,512]{3,2,1,0:T(8,128)(2,1)S(1)} %gather_fusion), kind=kOutput, calls=%fused_computation.11 | convolution fusion | flops 10771496960 | bytes 31723520 | tf_op jit(solution)/shard_map/dot_general | solution.py:117
  277.1 0.2 fusion.25
  277.3 0.0 copy-start.1
  277.3 0.2 multiply_subtract_fusion
  277.5 0.1 pad_maximum_fusion
  277.6 0.3 fusion.4
  277.9 2.1 copy.55
  (22 shorter events, 0.2 us)
Async XLA Ops:
  6.5 3.1 %copy-start = (bf16[256,4096]{1,0:T(8,128)(2,1)S(1)}, bf16[256,4096]{1,0:T(8,128)(2,1)}, u32[]{:S(2)}) copy-start(bf16[256,4096]{1,0:T(8,128)(2,1)} %param.8) | copy-start | bytes 6291460
  12.8 110.4 %all-to-all-start = ((bf16[16,32,4096]{2,1,0:T(8,128)(2,1)}), bf16[16,32,4096]{2,1,0:T(8,128)(2,1)}, u32[]{:S(2)}, u32[]{:S(2)}) async-start(bf16[16,32,4096]{2,1,0:T(8,128)(2,1)} %bitcast.77), calls=%async_computation | async-start | bytes 8388608 | tf_op jit(solution)/shard_map/all_to_all | solution.py:114
  20.3 103.0 %copy-start.4 = (bf16[2,512]{1,0:T(2,128)(2,1)S(1)}, bf16[2,512]{1,0:T(2,128)(2,1)}, u32[]{:S(2)}) copy-start(bf16[2,512]{1,0:T(2,128)(2,1)} %param.10) | copy-start | bytes 6148
  20.3 103.0 %copy-start.5 = (s32[1,8]{1,0:T(1,128)S(1)}, s32[1,8]{1,0:T(1,128)}, u32[]{:S(2)}) copy-start(s32[1,8]{1,0:T(1,128)} %param.14) | copy-start | bytes 100
  20.3 138.4 %copy-start.3 = (s32[256]{0:T(256)S(1)}, s32[256]{0:T(256)}, u32[]{:S(2)}) copy-start(s32[256]{0:T(256)} %param.15) | copy-start | bytes 3076
  20.3 220.1 %all-gather.7.cloned.1.call-start = ((), (), s32[]{:S(2)}) async-start(), calls=%async_computation.2 | async-start | bytes 4456448 | tf_op jit(solution)/shard_map/all_gather | solution.py:85
  21.0 236.6 %all-gather.5.cloned.1.call-start = ((), (), s32[]{:S(2)}) async-start(), calls=%async_computation.1 | async-start | bytes 12582912 | tf_op jit(solution)/shard_map/all_gather | solution.py:118
  178.0 41.0 %copy-start.6 = (s32[16]{0:T(128)S(1)}, s32[16]{0:T(128)}, u32[]{:S(2)}) copy-start(s32[16]{0:T(128)} %param.13) | copy-start | bytes 196
  178.0 41.7 %copy-start.2 = (bf16[2,8,512]{2,1,0:T(8,128)(2,1)S(1)}, bf16[2,8,512]{2,1,0:T(8,128)(2,1)}, u32[]{:S(2)}) copy-start(bf16[2,8,512]{2,1,0:T(8,128)(2,1)} %param.12) | copy-start | bytes 49156
  277.3 2.7 copy-start.1
Sparse Core Ops, SparseCore 0:
  23.3 93.8 all-gather.6
  123.4 118.9 all-gather.4
where the time goes:
time: 288 us; the launch traced here: 287 us
  waiting for transfers between devices  103 us (36%)
  blocking collectives  72.2 us (25%)
  local copies, waits for them, and re-layouts  62.5 us (22%)
  matrix products  22.7 us (8%)
  between operations  13.6 us (5%)
  starting transfers between devices  7.51 us (3%)
  other arithmetic  5.5 us (2%)
    all_to_all x1, waiting for transfers between devices, body(): lax.all_to_all(outgoing, 'rollout', split_axis=0, concat_axis=0, tiled=True)  102 us
    unnamed x15, local copies, waits for them, and re-layouts  41.1 us
    all_gather x1, blocking collectives, body(): lax.all_gather(lengths, 'rollout', axis=0, tiled=True)  35.2 us
    all_gather x1, blocking collectives, body(): lax.all_gather(adapter_up_blocks, 'rollout', axis=1, tiled=True)  19.5 us
    dot_general x1, matrix products, body(): jnp.dot(lax.all_gather(arrived, 'tensor', axis=1, tiled=True), merged_fla...  19.5 us
    all_gather x1, blocking collectives, body(): lax.all_gather(routes, 'rollout', axis=0, tiled=True)  17.4 us
    gather x2, local copies, waits for them, and re-layouts, body(): down_persisted.reshape(group_count, row_block_size, 2, -1)  17.3 us
    all_to_all x1, starting transfers between devices, body(): lax.all_to_all(outgoing, 'rollout', split_axis=0, concat_axis=0, tiled=True)  7.43 us
  transfers between devices with their start and end apart: 3, of which 1 were waited for; matrix products, arithmetic and copies ran while one was open for 22% of the time, Pallas kernels for 0%

commit v1 on v0

v1 whole, which is shorter than its diff:
```python
import jax
import jax.numpy as jnp
from jax import lax
from jax.sharding import PartitionSpec as P

HEAD = 128


adapter_scale = 2.0
rope_base = 1000000.0


def positions_of(lengths_row, row_count):
    ends = jnp.cumsum(lengths_row)
    starts = ends - lengths_row
    index = jnp.arange(row_count, dtype=jnp.int32)
    begins = jnp.max(jnp.where(starts[None, :] <= index[:, None], starts[None, :], 0), axis=1)
    return index - begins


def rotate(keys, places):
    half_width = HEAD // 2
    frequency = rope_base ** (-(jnp.arange(half_width, dtype=jnp.float32) * 2.0) / HEAD)
    angles = places.astype(jnp.float32)[:, None] * frequency[None, :]
    cosine = jnp.cos(angles)[:, None, :]
    sine = jnp.sin(angles)[:, None, :]
    shaped = keys.reshape(keys.shape[0], -1, HEAD)
    first = shaped[..., :half_width]
    second = shaped[..., half_width:]
    turned = jnp.concatenate(
        [first * cosine - second * sine, second * cosine + first * sine], axis=-1
    )
    return turned.reshape(keys.shape)


def slot_index(target, group_count, capacity):
    matches = (target[:, None] == jnp.arange(group_count, dtype=jnp.int32)[None, :]).astype(
        jnp.int32
    )
    order_in = jnp.sum((jnp.cumsum(matches, axis=0) - matches) * matches, axis=1)
    return target * capacity + order_in


def body(
    tokens,
    base_key_value_weight,
    key_value_bias,
    adapter_down_blocks,
    adapter_up_blocks,
    owner_shard_lookup,
    lengths,
    routes,
):
    group_count = lax.axis_size("rollout")
    row_count = tokens.shape[0]
    capacity = 2 * row_count // group_count
    width = base_key_value_weight.shape[2]
    model_width = base_key_value_weight.shape[0]
    inverse_permutation = (
        jnp.zeros((group_count,), jnp.int32)
        .at[owner_shard_lookup]
        .set(jnp.arange(group_count, dtype=jnp.int32))
    )
    up_persisted = lax.all_gather(adapter_up_blocks, "rollout", axis=0, tiled=False)
    down_persisted = lax.all_gather(adapter_down_blocks, "rollout", axis=0, tiled=False)
    rows = lax.all_gather(tokens, "tensor", axis=1, tiled=True)
    down = down_persisted[inverse_permutation].reshape(model_width, -1)
    up = up_persisted[inverse_permutation].transpose(1, 0, 2, 3).reshape(2, -1, width)
    rank = up.shape[1]
    low = jnp.dot(rows, down, preferred_element_type=jnp.float32)
    low = (adapter_scale * low).astype(jnp.bfloat16).reshape(row_count, 2, rank)
    update = jnp.einsum("nsr,src->nsc", low, up, preferred_element_type=jnp.float32)
    summed = jnp.einsum(
        "nf,fsc->nsc", rows, base_key_value_weight, preferred_element_type=jnp.float32
    )
    shaped = summed + update + key_value_bias.astype(jnp.float32)[None]
    places = positions_of(lengths[0], row_count)
    keys = rotate(shaped[:, 0], places)
    finished = jnp.concatenate([keys, shaped[:, 1]], axis=1).astype(jnp.bfloat16)
    slot_count = group_count * capacity
    send_slots = slot_index(routes, group_count, capacity)
    selector = (jnp.arange(slot_count, dtype=jnp.int32)[:, None] == send_slots[None, :]).astype(
        jnp.bfloat16
    )
    outgoing = jnp.dot(selector, finished, preferred_element_type=jnp.float32).astype(jnp.bfloat16)
    arrived = lax.all_to_all(
        outgoing.reshape(group_count, capacity, 2 * width),
        "rollout",
        split_axis=0,
        concat_axis=0,
        tiled=True,
    )
    return arrived.reshape(slot_count, 2, width)


def solution(mesh):
    in_specs = (
        P("rollout", "tensor"),
        P(None, None, "tensor"),
        P(None, "tensor"),
        P("rollout", None, None),
        P(None, "rollout", "tensor"),
        P(),
        P("rollout", None),
        P("rollout"),
    )
    out_specs = P("rollout", None, "tensor")
    return jax.shard_map(body, mesh=mesh, in_specs=in_specs, out_specs=out_specs, check_vma=False)
```

time: 288 us -> 177 us (0.61)
  the two profiles are of different devices: /device:TPU:0 before, /device:TPU:15 now
where the time goes in v1:
time: 177 us; the launch traced here: 175 us
  waiting for transfers between devices  78.8 us (45%)
  blocking collectives  45.6 us (26%)
  local copies, waits for them, and re-layouts  15.4 us (9%)
  matrix products  15 us (8%)
  between operations  13.5 us (8%)
  other arithmetic  7.1 us (4%)
    all_gather x1, waiting for transfers between devices, body(): lax.all_gather(adapter_down_blocks, 'rollout', axis=0, tiled=False)  43.8 us
    all_gather x1, waiting for transfers between devices, body(): rows = lax.all_gather(tokens, 'tensor', axis=1, tiled=True)  33.7 us
    all_to_all x1, blocking collectives, body(): lax.all_to_all(outgoing.reshape(group_count, capacity, 2 * width), 'rollo...  29.1 us
    all_gather x1, blocking collectives, body(): lax.all_gather(adapter_up_blocks, 'rollout', axis=0, tiled=False)  16.6 us
    gather x1, local copies, waits for them, and re-layouts, body(): down = down_persisted[inverse_permutation].reshape(model_width, -1)  12.1 us
    dot_general x1, matrix products, body(): jnp.einsum('nf,fsc->nsc', rows, base_key_value_weight, preferred_element_...  9.4 us
    dot_general x1, matrix products, body(): low = jnp.dot(rows, down, preferred_element_type=jnp.float32)  4.77 us
  transfers between devices with their start and end apart: 2, of which 2 were waited for; matrix products, arithmetic and copies ran while one was open for 10% of the time, Pallas kernels for 0%

profile of v1, /device:TPU:15, one launch (start us, length us, event | category | flops | bytes accessed | tf_op | source)
XLA Modules:
  0.0 175.4 jit_solution(5785317210339361498)
XLA Ops:
  6.5 0.0 all-gather.5.cloned.1.call-start
  6.5 0.7 all-gather.5.cloned.1.call-update
  7.3 0.0 all-gather.7.cloned.1.call-start
  7.3 0.7 all-gather.7.cloned.1.call-update
  8.0 0.7 convert_element_type.32
  8.7 0.8 reduce-window_2_clone.1
  9.5 0.7 fusion.24
  10.2 0.6 reduce-window.9
  10.8 0.2 slice_reduce_fusion
  11.0 0.7 compare_select_fusion.1
  11.7 0.6 scatter_custom_fusion
  12.3 16.6 %all-gather = bf16[32,8,512]{2,1,0:T(8,128)(2,1)S(1)} all-gather(bf16[2,8,512]{2,1,0:T(8,128)(2,1)} %param.12), channel_id=2, replica_groups=mesh['rollout'=16,'tensor'=2] {'rollout'}, dimensions={0}, use_global_device_ids=true | all-gather | bytes 278528 | tf_op jit(solution)/shard_map/all_gather | solution.py:64
  28.9 0.6 gather_fusion
  29.5 0.7 subtract_bitcast_fusion
  30.1 0.1 select_reduce_fusion
  30.2 0.8 fusion.23
  31.0 0.7 multiply_add_fusion
  31.7 0.5 multiply_cosine_fusion
  32.2 33.7 %all-gather.5.cloned.1.call-done = bf16[256,8192]{1,0:T(8,128)(2,1)} async-done(((bf16[256,4096]{1,0:T(8,128)(2,1)}), bf16[256,8192]{1,0:T(8,128)(2,1)}) %all-gather.5.cloned.1.call-update) | async-done | bytes 4194320 | tf_op jit(solution)/shard_map/all_gather | solution.py:66
  65.9 9.4 %fusion = f32[256,2,512]{2,0,1:T(8,128)S(1)} fusion(bf16[8192,2,512]{2,1,0:T(2,128)(2,1)} %param.9, bf16[256,8192]{1,0:T(8,128)(2,1)} %all-gather.5.cloned.1.call-done), kind=kOutput, calls=%fused_computation.3 | convolution fusion | flops 4294967296 | bytes 22020096 | tf_op jit(solution)/shard_map/nf,fsc->nsc/dot_general | solution.py:73
  75.3 43.8 %all-gather.7.cloned.1.call-done = bf16[8192,2,128]{2,1,0:T(2,128)(2,1)} async-done(((bf16[512,2,128]{2,1,0:T(2,128)(2,1)}), bf16[8192,2,128]{2,1,0:T(2,128)(2,1)}) %all-gather.7.cloned.1.call-update) | async-done | bytes 4194320 | tf_op jit(solution)/shard_map/all_gather | solution.py:65
  119.0 12.1 %gather_fusion.1 = bf16[16,512,2,128]{3,2,1,0:T(2,128)(2,1)} fusion(bf16[16,512,2,128]{3,2,1,0:T(2,128)(2,1)} %bitcast.63, s32[1024]{0:T(1024)S(1)} %pad_clamp_fusion), kind=kCustom, calls=%fused_computation.1 | custom fusion | bytes 8388672 | tf_op jit(solution)/shard_map/gather | solution.py:67
  131.2 4.8 %fusion.11 = bf16[256,256]{1,0:T(8,128)(2,1)S(1)} fusion(bf16[256,8192]{1,0:T(8,128)(2,1)} %all-gather.5.cloned.1.call-done, bf16[1024,8,2,128]{3,2,1,0:T(2,128)(2,1)} %bitcast.64), kind=kOutput, calls=%fused_computation.14 | convolution fusion | flops 1073872896 | bytes 8519680 | tf_op jit(solution)/shard_map/dot_general | solution.py:70
  136.0 0.3 fusion.7
  136.4 0.2 reshape_squeeze.3
  136.6 0.5 subtract_convert_fusion
  137.1 0.4 pad_maximum_fusion
  137.5 0.4 convolution_convert_fusion
  138.0 29.1 %all_to_all.5 = bf16[16,32,1024]{2,1,0:T(8,128)(2,1)S(1)} all-to-all(bf16[16,32,1024]{2,1,0:T(8,128)(2,1)S(1)} %bitcast.67), channel_id=1, replica_groups=mesh['rollout'=16,'tensor'=2] {'rollout'}, dimensions={0} | all-to-all | bytes 2097152 | tf_op jit(solution)/shard_map/all_to_all | solution.py:86
  167.0 1.6 reshape.110
  (10 shorter events, 0.2 us)
Async XLA Ops:
  6.5 59.3 %all-gather.5.cloned.1.call-start = ((), (), s32[]{:S(2)}) async-start(), calls=%async_computation.1 | async-start | bytes 6291456 | tf_op jit(solution)/shard_map/all_gather | solution.py:66
  7.3 111.8 %all-gather.7.cloned.1.call-start = ((), (), s32[]{:S(2)}) async-start(), calls=%async_computation.2 | async-start | bytes 4456448 | tf_op jit(solution)/shard_map/all_gather | solution.py:65
Sparse Core Ops, SparseCore 0:
  8.9 56.9 all-gather.4
  68.0 50.9 all-gather.6

commit v2 on v1

--- a/solution.py
+++ b/solution.py
@@ -1,6 +1,10 @@
+import functools
+
 import jax
 import jax.numpy as jnp
 from jax import lax
+from jax.experimental import pallas as pl
+from jax.experimental.pallas import tpu as pltpu
 from jax.sharding import PartitionSpec as P
 
 HEAD = 128
@@ -39,6 +43,195 @@
     )
     order_in = jnp.sum((jnp.cumsum(matches, axis=0) - matches) * matches, axis=1)
     return target * capacity + order_in
+
+
+def gather_kernel(
+    groups,
+    shards,
+    tokens,
+    factors,
+    rows_out,
+    factors_out,
+    local_sem,
+    token_send,
+    token_recv,
+    factor_send,
+    factor_recv,
+    forward_send,
+    forward_recv,
+):
+    me = lax.axis_index("rollout")
+    part = lax.axis_index("tensor")
+    chips = groups // 2
+    chip, core = me // 2, me % 2
+    sibling = chip * 2 + (1 - core)
+    features = tokens.shape[1]
+
+    def same_core(step):
+        return ((chip + step + chips) % chips) * 2 + core
+
+    barrier = pltpu.get_barrier_semaphore()
+    for step in range(1, shards):
+        pl.semaphore_signal(barrier, inc=1, device_id={"tensor": (part + step) % shards})
+    for step in range(1, chips):
+        pl.semaphore_signal(barrier, inc=1, device_id={"rollout": same_core(step)})
+    pl.semaphore_signal(barrier, inc=1, device_id={"rollout": sibling})
+    pl.semaphore_wait(barrier, shards - 1 + chips - 1 + 1)
+
+    columns = pl.ds(pl.multiple_of(part * features, features), features)
+    copies = []
+    for step in range(1, shards):
+        copies.append(
+            pltpu.make_async_remote_copy(
+                src_ref=tokens,
+                dst_ref=rows_out.at[:, columns],
+                send_sem=token_send.at[step],
+                recv_sem=token_recv.at[step],
+                device_id={"tensor": (part + step) % shards},
+            )
+        )
+        copies[-1].start()
+    sends = []
+    for step in range(1, chips):
+        sends.append(
+            pltpu.make_async_remote_copy(
+                src_ref=factors,
+                dst_ref=factors_out.at[me],
+                send_sem=factor_send.at[step],
+                recv_sem=factor_recv.at[step],
+                device_id={"rollout": same_core(step)},
+            )
+        )
+        sends[-1].start()
+    copies.append(
+        pltpu.make_async_remote_copy(
+            src_ref=factors,
+            dst_ref=factors_out.at[me],
+            send_sem=forward_send.at[0],
+            recv_sem=forward_recv.at[0],
+            device_id={"rollout": sibling},
+        )
+    )
+    copies[-1].start()
+    own_rows = pltpu.make_async_copy(tokens, rows_out.at[:, columns], local_sem.at[0])
+    own_rows.start()
+    own_factors = pltpu.make_async_copy(factors, factors_out.at[me], local_sem.at[1])
+    own_factors.start()
+    for step in range(1, chips):
+        sends[step - 1].wait_recv()
+        source = same_core(-step)
+        copies.append(
+            pltpu.make_async_remote_copy(
+                src_ref=factors_out.at[source],
+                dst_ref=factors_out.at[source],
+                send_sem=forward_send.at[step],
+                recv_sem=forward_recv.at[step],
+                device_id={"rollout": sibling},
+            )
+        )
+        copies[-1].start()
+    for copy in sends:
+        copy.wait_send()
+    for copy in copies:
+        copy.wait()
+    own_rows.wait()
+    own_factors.wait()
+
+
+def gather_all(tokens, factors, groups, shards):
+    chips = groups // 2
+    rows, features = tokens.shape
+    dma = pltpu.SemaphoreType.DMA
+    return pl.pallas_call(
+        functools.partial(gather_kernel, groups, shards),
+        out_shape=(
+            jax.ShapeDtypeStruct((rows, shards * features), tokens.dtype),
+            jax.ShapeDtypeStruct((groups,) + factors.shape, factors.dtype),
+        ),
+        in_specs=[pl.BlockSpec(memory_space=pl.ANY)] * 2,
+        out_specs=[pl.BlockSpec(memory_space=pl.ANY)] * 2,
+        scratch_shapes=[
+            dma((2,)),
+            dma((shards,)),
+            dma((shards,)),
+            dma((chips,)),
+            dma((chips,)),
+            dma((chips,)),
+            dma((chips,)),
+        ],
+        compiler_params=pltpu.CompilerParams(collective_id=0, has_side_effects=True),
+    )(tokens, factors)
+
+
+def exchange_kernel(groups, outgoing, arrived, local_sem, send_sem, recv_sem):
+    me = lax.axis_index("rollout")
+    barrier = pltpu.get_barrier_semaphore()
+    for step in range(1, groups):
+        pl.semaphore_signal(barrier, inc=1, device_id={"rollout": (me + step) % groups})
+    pl.semaphore_wait(barrier, groups - 1)
+    copies = []
+    for step in range(1, groups):
+        peer = (me + step) % groups
+        copies.append(
+            pltpu.make_async_remote_copy(
+                src_ref=outgoing.at[peer],
+                dst_ref=arrived.at[me],
+                send_sem=send_sem.at[step],
+                recv_sem=recv_sem.at[step],
+                device_id={"rollout": peer},
+            )
+        )
+        copies[-1].start()
+    own = pltpu.make_async_copy(outgoing.at[me], arrived.at[me], local_sem)
+    own.start()
+    for copy in copies:
+        copy.wait()
+    own.wait()
+
+
+def exchange(outgoing, groups):
+    dma = pltpu.SemaphoreType.DMA
+    return pl.pallas_call(
+        functools.partial(exchange_kernel, groups),
+        out_shape=jax.ShapeDtypeStruct(outgoing.shape, outgoing.dtype),
+        in_specs=[pl.BlockSpec(memory_space=pl.ANY)],
+        out_specs=pl.BlockSpec(memory_space=pl.ANY),
+        scratch_shapes=[dma, dma((groups,)), dma((groups,))],
+        compiler_params=pltpu.CompilerParams(collective_id=1, has_side_effects=True),
+    )(outgoing)
+
+
+def low_kernel(lookup, rows, down, low, total):
+    step = pl.program_id(0)
+
+    @pl.when(step == 0)
+    def _():
+        total[...] = jnp.zeros_like(total)
+
+    total[...] += jnp.dot(rows[...], down[0], preferred_element_type=jnp.float32)
+
+    @pl.when(step == pl.num_programs(0) - 1)
+    def _():
+        low[...] = (adapter_scale * total[...]).astype(low.dtype)
+
+
+def low_rank(lookup, rows, factors, block_rows):
+    row_count = rows.shape[0]
+    groups, _, columns = factors.shape
+    return pl.pallas_call(
+        low_kernel,
+        out_shape=jax.ShapeDtypeStruct((row_count, columns), jnp.bfloat16),
+        grid_spec=pltpu.PrefetchScalarGridSpec(
+            num_scalar_prefetch=1,
+            grid=(groups,),
+            in_specs=[
+                pl.BlockSpec((row_count, block_rows), lambda i, lookup: (0, lookup[i])),
+                pl.BlockSpec((1, block_rows, columns), lambda i, lookup: (i, 0, 0)),
+            ],
+            out_specs=pl.BlockSpec((row_count, columns), lambda i, lookup: (0, 0)),
+            scratch_shapes=[pltpu.VMEM((row_count, columns), jnp.float32)],
+        ),
+    )(lookup, rows, factors)
 
 
 def body(
@@ -55,20 +248,25 @@
     row_count = tokens.shape[0]
     capacity = 2 * row_count // group_count
     width = base_key_value_weight.shape[2]
-    model_width = base_key_value_weight.shape[0]
     inverse_permutation = (
         jnp.zeros((group_count,), jnp.int32)
         .at[owner_shard_lookup]
         .set(jnp.arange(group_count, dtype=jnp.int32))
     )
-    up_persisted = lax.all_gather(adapter_up_blocks, "rollout", axis=0, tiled=False)
-    down_persisted = lax.all_gather(adapter_down_blocks, "rollout", axis=0, tiled=False)
-    rows = lax.all_gather(tokens, "tensor", axis=1, tiled=True)
-    down = down_persisted[inverse_permutation].reshape(model_width, -1)
-    up = up_persisted[inverse_permutation].transpose(1, 0, 2, 3).reshape(2, -1, width)
-    rank = up.shape[1]
-    low = jnp.dot(rows, down, preferred_element_type=jnp.float32)
-    low = (adapter_scale * low).astype(jnp.bfloat16).reshape(row_count, 2, rank)
+    block_rows = adapter_down_blocks.shape[0]
+    low_width = 2 * adapter_down_blocks.shape[2]
+    factors = jnp.concatenate(
+        [
+            adapter_down_blocks.reshape(block_rows, low_width),
+            adapter_up_blocks.reshape(-1, low_width),
+        ],
+        axis=0,
+    )
+    rows, all_factors = gather_all(tokens, factors, group_count, lax.axis_size("tensor"))
+    low = low_rank(owner_shard_lookup, rows, all_factors, block_rows)
+    low = low.reshape(row_count, 2, -1)
+    up_blocks = all_factors[:, block_rows:].reshape((group_count,) + adapter_up_blocks.shape)
+    up = up_blocks[inverse_permutation].transpose(1, 0, 2, 3).reshape(2, -1, width)
     update = jnp.einsum("nsr,src->nsc", low, up, preferred_element_type=jnp.float32)
     summed = jnp.einsum(
         "nf,fsc->nsc", rows, base_key_value_weight, preferred_element_type=jnp.float32
@@ -83,13 +281,7 @@
         jnp.bfloat16
     )
     outgoing = jnp.dot(selector, finished, preferred_element_type=jnp.float32).astype(jnp.bfloat16)
-    arrived = lax.all_to_all(
-        outgoing.reshape(group_count, capacity, 2 * width),
-        "rollout",
-        split_axis=0,
-        concat_axis=0,
-        tiled=True,
-    )
+    arrived = exchange(outgoing.reshape(group_count, capacity, 2 * width), group_count)
     return arrived.reshape(slot_count, 2, width)
 
 

time: 177 us -> 143 us (0.81)
  Pallas kernels: 0 us -> 116 us
  waiting for transfers between devices: 78.8 us -> 0 us
  blocking collectives: 45.6 us -> 0 us
  between operations: 13.5 us -> 0.16 us
  local copies, waits for them, and re-layouts: 15.4 us -> 7.07 us
  matrix products: 15 us -> 11.1 us
    pallas_call x0 -> x3, Pallas kernels: none -> 116 us  [the longest x1 75.7 us: gather_all(): pl.pallas_call(functools.partial(gather_kernel, groups, shards), out_shap...]
    all_gather x2 -> x0, waiting for transfers between devices: 77.4 us -> none  [the longest x1 43.8 us: body(): lax.all_gather(adapter_down_blocks, 'rollout', axis=0, tiled=False)]
    all_to_all x1 -> x0, blocking collectives: 29.1 us -> none  [body(): lax.all_to_all(outgoing.reshape(group_count, capacity, 2 * width), 'rollo...]
    all_gather x1 -> x0, blocking collectives: 16.6 us -> none  [body(): lax.all_gather(adapter_up_blocks, 'rollout', axis=0, tiled=False)]
    gather x2 -> x1, local copies, waits for them, and re-layouts: 12.7 us -> 0.56 us  [body(): up_blocks[inverse_permutation].transpose(1, 0, 2, 3).reshape(2, -1, width)]
    dot_general x1 -> x0, matrix products: 4.77 us -> none  [body(): low = jnp.dot(rows, down, preferred_element_type=jnp.float32)]
  transfers between devices with their start and end apart: 2 -> 0, of which waited for: 2 -> 0; matrix products, arithmetic and copies ran while one was open for 10% -> 0% of each run, Pallas kernels for 0% -> 0%
where the time goes in v2:
time: 143 us; the launch traced here: 142 us
  Pallas kernels  116 us (81%)
  matrix products  11.1 us (8%)
  other arithmetic  7.83 us (5%)
  local copies, waits for them, and re-layouts  7.07 us (5%)
    pallas_call x1, Pallas kernels, gather_all(): pl.pallas_call(functools.partial(gather_kernel, groups, shards), out_shap...  75.7 us
    pallas_call x1, Pallas kernels, exchange(): pl.pallas_call(functools.partial(exchange_kernel, groups), out_shape=jax....  28.3 us
    pallas_call x1, Pallas kernels, low_rank(): pl.pallas_call(low_kernel, out_shape=jax.ShapeDtypeStruct((row_count, col...  12.1 us
    dot_general x1, matrix products, body(): jnp.einsum('nf,fsc->nsc', rows, base_key_value_weight, preferred_element_...  9.41 us

profile of v2, /device:TPU:15, one launch (start us, length us, event | category | flops | bytes accessed | tf_op | source)
XLA Modules:
  0.0 142.2 jit_solution(18388741117954123478)
XLA Ops:
  0.0 0.7 compare_select_fusion.1
  0.7 0.8 reduce-window_2_clone.1
  1.5 0.7 subtract_bitcast_fusion
  2.1 0.1 select_reduce_fusion
  2.3 0.6 scatter_custom_fusion
  2.9 0.7 convert_element_type.24
  3.6 0.7 reshape.112
  4.3 0.7 fusion.17
  5.0 0.6 reduce-window.9
  5.6 0.2 slice_reduce_fusion
  5.8 0.8 fusion.16
  6.6 0.7 multiply_add_fusion
  7.3 0.5 multiply_cosine_fusion
  7.8 1.0 copy.50
  8.8 0.7 pad_maximum_fusion.factors
  9.5 75.7 %shard_map.82 = (bf16[256,8192]{1,0:T(8,128)(2,1)}, bf16[16,544,256]{2,1,0:T(8,128)(2,1)}) custom-call(bf16[256,4096]{1,0:T(8,128)(2,1)} %tokens.1, bf16[544,256]{1,0:T(8,128)(2,1)} %pad_maximum_fusion.factors), custom_call_target="tpu_custom_call" | custom-call | tf_op jit(solution)/shard_map/pallas_call | solution.py:145
  85.3 12.1 %shard_map.83 = bf16[256,256]{1,0:T(8,128)(2,1)} custom-call(s32[16]{0:T(128)} %lookup.1, bf16[256,8192]{1,0:T(8,128)(2,1)} %get-tuple-element.7.rows, bf16[16,544,256]{2,1,0:T(8,128)(2,1)} %get-tuple-element.8.down), custom_call_target="tpu_custom_call" | custom-call | tf_op jit(solution)/shard_map/pallas_call | solution.py:221
  97.3 1.0 slice.24
  98.3 0.0 copy-start
  98.3 9.4 %fusion = f32[256,2,512]{2,0,1:T(8,128)S(1)} fusion(bf16[8192,2,512]{2,1,0:T(2,128)(2,1)} %param.9, bf16[256,8192]{1,0:T(8,128)(2,1)} %get-tuple-element.7.rows), kind=kOutput, calls=%fused_computation.2 | convolution fusion | flops 4294967296 | bytes 22020096 | tf_op jit(solution)/shard_map/nf,fsc->nsc/dot_general | solution.py:271
  107.7 0.1 reshape.113
  107.8 0.6 gather_fusion
  108.4 0.0 copy-done
  108.4 0.3 fusion.4
  108.8 0.2 reshape_squeeze.3
  109.0 0.5 subtract_convert_fusion
  109.5 0.4 pad_maximum_fusion.1
  109.9 1.4 convolution_convert_fusion
  111.3 28.3 %shard_map.84 = bf16[16,32,1024]{2,1,0:T(8,128)(2,1)} custom-call(bf16[16,32,1024]{2,1,0:T(8,128)(2,1)} %bitcast.60), custom_call_target="tpu_custom_call" | custom-call | tf_op jit(solution)/shard_map/pallas_call | solution.py:194
  139.6 2.6 %reshape.118 = bf16[512,2,512]{2,1,0:T(2,128)(2,1)} reshape(bf16[16,32,1024]{2,1,0:T(8,128)(2,1)} %shard_map.84) | data formatting | bytes 2097152 | tf_op jit(solution)/shard_map/reshape | solution.py:285
  (10 shorter events, 0.2 us)
Async XLA Ops:
  98.3 10.1 %copy-start = (bf16[256,256]{1,0:T(8,128)(2,1)S(1)}, bf16[256,256]{1,0:T(8,128)(2,1)}, u32[]{:S(2)}) copy-start(bf16[256,256]{1,0:T(8,128)(2,1)} %shard_map.83) | copy-start | bytes 393220

commit v3 on v2

v3 whole, which is shorter than its diff:
```python
import functools

import jax
import jax.numpy as jnp
from jax import lax
from jax.experimental import pallas as pl
from jax.experimental.pallas import tpu as pltpu
from jax.sharding import PartitionSpec as P

HEAD = 128


adapter_scale = 2.0
rope_base = 1000000.0


def positions_of(lengths_row, row_count):
    ends = jnp.cumsum(lengths_row)
    starts = ends - lengths_row
    index = jnp.arange(row_count, dtype=jnp.int32)
    begins = jnp.max(jnp.where(starts[None, :] <= index[:, None], starts[None, :], 0), axis=1)
    return index - begins


def rotate(keys, places):
    half_width = HEAD // 2
    frequency = rope_base ** (-(jnp.arange(half_width, dtype=jnp.float32) * 2.0) / HEAD)
    angles = places.astype(jnp.float32)[:, None] * frequency[None, :]
    cosine = jnp.cos(angles)[:, None, :]
    sine = jnp.sin(angles)[:, None, :]
    shaped = keys.reshape(keys.shape[0], -1, HEAD)
    first = shaped[..., :half_width]
    second = shaped[..., half_width:]
    turned = jnp.concatenate(
        [first * cosine - second * sine, second * cosine + first * sine], axis=-1
    )
    return turned.reshape(keys.shape)


def slot_index(target, group_count, capacity):
    matches = (target[:, None] == jnp.arange(group_count, dtype=jnp.int32)[None, :]).astype(
        jnp.int32
    )
    order_in = jnp.sum((jnp.cumsum(matches, axis=0) - matches) * matches, axis=1)
    return target * capacity + order_in


CHUNKS = 4


def gather_kernel(
    groups,
    shards,
    inverse,
    tokens,
    down,
    up,
    rows_out,
    low_out,
    up_out,
    down_all,
    local_sem,
    token_send,
    token_recv,
    down_send,
    down_recv,
    up_send,
    up_recv,
    forward_send,
    forward_recv,
    low_send,
    low_recv,
):
    me = lax.axis_index("rollout")
    part = lax.axis_index("tensor")
    chips = groups // 2
    chip, core = me // 2, me % 2
    sibling = chip * 2 + (1 - core)
    row_count, features = tokens.shape
    block_rows = down.shape[0]

    def same_core(step):
        return ((chip + step + chips) % chips) * 2 + core

    barrier = pltpu.get_barrier_semaphore()
    for step in range(1, shards):
        pl.semaphore_signal(barrier, inc=1, device_id={"tensor": (part + step) % shards})
    for step in range(1, groups):
        pl.semaphore_signal(barrier, inc=1, device_id={"rollout": (me + step) % groups})
    pl.semaphore_wait(barrier, shards - 1 + groups - 1)

    columns = pl.ds(pl.multiple_of(part * features, features), features)
    chunk_rows = row_count // CHUNKS
    copies = []
    sends = []
    for step in range(1, chips):
        sends.append(
            pltpu.make_async_remote_copy(
                src_ref=down,
                dst_ref=down_all.at[me],
                send_sem=down_send.at[step],
                recv_sem=down_recv.at[step],
                device_id={"rollout": same_core(step)},
            )
        )
        sends[-1].start()
    for chunk in range(CHUNKS):
        for step in range(1, shards):
            piece = pl.ds(chunk * chunk_rows, chunk_rows)
            copies.append(
                pltpu.make_async_remote_copy(
                    src_ref=tokens.at[piece],
                    dst_ref=rows_out.at[piece, columns],
                    send_sem=token_send.at[step, chunk],
                    recv_sem=token_recv.at[step, chunk],
                    device_id={"tensor": (part + step) % shards},
                )
            )
            copies[-1].start()
    copies.append(
        pltpu.make_async_remote_copy(
            src_ref=down,
            dst_ref=down_all.at[me],
            send_sem=forward_send.at[0],
            recv_sem=forward_recv.at[0],
            device_id={"rollout": sibling},
        )
    )
    copies[-1].start()
    for step in range(1, groups):
        copies.append(
            pltpu.make_async_remote_copy(
                src_ref=up,
                dst_ref=up_out.at[me],
                send_sem=up_send.at[step],
                recv_sem=up_recv.at[step],
                device_id={"rollout": (me + step) % groups},
            )
        )
        copies[-1].start()
    own = [
        pltpu.make_async_copy(tokens, rows_out.at[:, columns], local_sem.at[0]),
        pltpu.make_async_copy(down, down_all.at[me], local_sem.at[1]),
        pltpu.make_async_copy(up, up_out.at[me], local_sem.at[2]),
    ]
    for copy in own:
        copy.start()
    for step in range(1, chips):
        sends[step - 1].wait_recv()
        source = same_core(-step)
        copies.append(
            pltpu.make_async_remote_copy(
                src_ref=down_all.at[source],
                dst_ref=down_all.at[source],
                send_sem=forward_send.at[step],
                recv_sem=forward_recv.at[step],
                device_id={"rollout": sibling},
            )
        )
        copies[-1].start()
    for copy in sends:
        copy.wait_send()
    for copy in copies:
        copy.wait()
    for copy in own:
        copy.wait()

    total = jnp.zeros(low_out.shape[1:], jnp.float32)
    for owner in range(groups):
        block = pl.ds(owner * block_rows, block_rows)
        factor = down_all[inverse[owner]]
        total += jnp.dot(rows_out[:, block], factor, preferred_element_type=jnp.float32)
    low_out[part] = (adapter_scale * total).astype(low_out.dtype)
    copies = []
    for step in range(1, shards):
        copies.append(
            pltpu.make_async_remote_copy(
                src_ref=low_out.at[part],
                dst_ref=low_out.at[part],
                send_sem=low_send.at[step],
                recv_sem=low_recv.at[step],
                device_id={"tensor": (part + step) % shards},
            )
        )
        copies[-1].start()
    for copy in copies:
        copy.wait()


def gather_all(inverse, tokens, down, up, groups, shards):
    chips = groups // 2
    rows, features = tokens.shape
    dma = pltpu.SemaphoreType.DMA
    vmem = pl.BlockSpec(memory_space=pltpu.VMEM)
    hbm = pl.BlockSpec(memory_space=pl.ANY)
    return pl.pallas_call(
        functools.partial(gather_kernel, groups, shards),
        out_shape=(
            jax.ShapeDtypeStruct((rows, shards * features), tokens.dtype),
            jax.ShapeDtypeStruct((shards, rows, down.shape[1]), jnp.bfloat16),
            jax.ShapeDtypeStruct((groups,) + up.shape, up.dtype),
        ),
        in_specs=[pl.BlockSpec(memory_space=pltpu.SMEM), hbm, vmem, vmem],
        out_specs=[vmem, vmem, vmem],
        scratch_shapes=[
            pltpu.VMEM((groups,) + down.shape, down.dtype),
            dma((3,)),
            dma((shards, CHUNKS)),
            dma((shards, CHUNKS)),
            dma((chips,)),
            dma((chips,)),
            dma((groups,)),
            dma((groups,)),
            dma((chips,)),
            dma((chips,)),
            dma((shards,)),
            dma((shards,)),
        ],
        compiler_params=pltpu.CompilerParams(
            collective_id=0, has_side_effects=True, vmem_limit_bytes=24 * 1024 * 1024
        ),
    )(inverse, tokens, down, up)


def exchange_kernel(groups, outgoing, arrived, local_sem, send_sem, recv_sem):
    me = lax.axis_index("rollout")
    barrier = pltpu.get_barrier_semaphore()
    for step in range(1, groups):
        pl.semaphore_signal(barrier, inc=1, device_id={"rollout": (me + step) % groups})
    pl.semaphore_wait(barrier, groups - 1)
    copies = []
    for step in range(1, groups):
        peer = (me + step) % groups
        copies.append(
            pltpu.make_async_remote_copy(
                src_ref=outgoing.at[peer],
                dst_ref=arrived.at[me],
                send_sem=send_sem.at[step],
                recv_sem=recv_sem.at[step],
                device_id={"rollout": peer},
            )
        )
        copies[-1].start()
    own = pltpu.make_async_copy(outgoing.at[me], arrived.at[me], local_sem)
    own.start()
    for copy in copies:
        copy.wait()
    own.wait()


def exchange(outgoing, groups):
    dma = pltpu.SemaphoreType.DMA
    return pl.pallas_call(
        functools.partial(exchange_kernel, groups),
        out_shape=jax.ShapeDtypeStruct(outgoing.shape, outgoing.dtype),
        in_specs=[pl.BlockSpec(memory_space=pl.ANY)],
        out_specs=pl.BlockSpec(memory_space=pl.ANY),
        scratch_shapes=[dma, dma((groups,)), dma((groups,))],
        compiler_params=pltpu.CompilerParams(collective_id=1, has_side_effects=True),
    )(outgoing)


def body(
    tokens,
    base_key_value_weight,
    key_value_bias,
    adapter_down_blocks,
    adapter_up_blocks,
    owner_shard_lookup,
    lengths,
    routes,
):
    group_count = lax.axis_size("rollout")
    row_count = tokens.shape[0]
    capacity = 2 * row_count // group_count
    width = base_key_value_weight.shape[2]
    order = jnp.arange(group_count, dtype=jnp.int32)
    inverse_permutation = jnp.sum(
        jnp.where(owner_shard_lookup[None, :] == order[:, None], order[None, :], 0), axis=1
    )
    block_rows = adapter_down_blocks.shape[0]
    shards = lax.axis_size("tensor")
    low_width = 2 * adapter_down_blocks.shape[2]
    down_part = lax.dynamic_slice_in_dim(
        adapter_down_blocks.reshape(block_rows, low_width),
        lax.axis_index("tensor") * (low_width // shards),
        low_width // shards,
        axis=1,
    )
    rows, low, up_blocks = gather_all(
        inverse_permutation,
        tokens,
        down_part,
        adapter_up_blocks.reshape(-1, width),
        group_count,
        shards,
    )
    low = low.transpose(1, 0, 2).reshape(row_count, 2, -1)
    up_blocks = up_blocks.reshape((group_count,) + adapter_up_blocks.shape)
    up = up_blocks[inverse_permutation].transpose(1, 0, 2, 3).reshape(2, -1, width)
    update = jnp.einsum("nsr,src->nsc", low, up, preferred_element_type=jnp.float32)
    summed = jnp.einsum(
        "nf,fsc->nsc", rows, base_key_value_weight, preferred_element_type=jnp.float32
    )
    shaped = summed + update + key_value_bias.astype(jnp.float32)[None]
    places = positions_of(lengths[0], row_count)
    keys = rotate(shaped[:, 0], places)
    finished = jnp.concatenate([keys, shaped[:, 1]], axis=1).astype(jnp.bfloat16)
    slot_count = group_count * capacity
    send_slots = slot_index(routes, group_count, capacity)
    selector = (jnp.arange(slot_count, dtype=jnp.int32)[:, None] == send_slots[None, :]).astype(
        jnp.bfloat16
    )
    outgoing = jnp.dot(selector, finished, preferred_element_type=jnp.float32).astype(jnp.bfloat16)
    arrived = exchange(outgoing.reshape(group_count, capacity, 2 * width), group_count)
    return arrived.reshape(slot_count, 2, width)


def solution(mesh):
    in_specs = (
        P("rollout", "tensor"),
        P(None, None, "tensor"),
        P(None, "tensor"),
        P("rollout", None, None),
        P(None, "rollout", "tensor"),
        P(),
        P("rollout", None),
        P("rollout"),
    )
    out_specs = P("rollout", None, "tensor")
    return jax.shard_map(body, mesh=mesh, in_specs=in_specs, out_specs=out_specs, check_vma=False)
```

time: 143 us -> 107 us (0.75)
  Pallas kernels: 116 us -> 83.5 us
  other arithmetic: 7.83 us -> 3.24 us
  local copies, waits for them, and re-layouts: 7.07 us -> 9 us
    pallas_call x1, Pallas kernels: 75.7 us -> 54.5 us  [gather_all(): pl.pallas_call(functools.partial(gather_kernel, groups, shards), out_shap...]
    pallas_call x1 -> x0, Pallas kernels: 12.1 us -> none  [low_rank(): pl.pallas_call(low_kernel, out_shape=jax.ShapeDtypeStruct((row_count, col...]
    unnamed x4 -> x14, local copies, waits for them, and re-layouts: 1.03 us -> 5.35 us
where the time goes in v3:
time: 107 us
  Pallas kernels  83.5 us (78%)
  matrix products  11.1 us (10%)
  local copies, waits for them, and re-layouts  9 us (8%)
  other arithmetic  3.24 us (3%)
    pallas_call x1, Pallas kernels, gather_all(): pl.pallas_call(functools.partial(gather_kernel, groups, shards), out_shap...  54.5 us
    pallas_call x1, Pallas kernels, exchange(): pl.pallas_call(functools.partial(exchange_kernel, groups), out_shape=jax....  29 us
    dot_general x1, matrix products, body(): jnp.einsum('nf,fsc->nsc', rows, base_key_value_weight, preferred_element_...  9.43 us
    unnamed x14, local copies, waits for them, and re-layouts  5.35 us
    reshape x1, local copies, waits for them, and re-layouts, body(): return arrived.reshape(slot_count, 2, width)  2.62 us

profile of v3, /device:TPU:15, one launch (start us, length us, event | category | flops | bytes accessed | tf_op | source)
XLA Modules:
  0.0 107.0 jit_solution(13650873383710568634)
XLA Ops:
  0.0 1.0 copy.41
  1.0 0.8 select_reduce_fusion.1.inverse
  1.8 0.0 copy-start
  1.8 1.6 %copy-done = bf16[256,4096]{1,0:T(8,128)(2,1)S(1)} copy-done((bf16[256,4096]{1,0:T(8,128)(2,1)S(1)}, bf16[256,4096]{1,0:T(8,128)(2,1)}, u32[]{:S(2)}) %copy-start) | copy-done | bytes 2097176
  3.4 0.0 copy-start.1
  3.4 0.7 copy-done.1
  4.1 54.5 %shard_map.82 = (bf16[256,8192]{1,0:T(8,128)(2,1)S(1)}, bf16[2,256,128]{2,1,0:T(8,128)(2,1)S(1)}, bf16[16,16,512]{2,1,0:T(8,128)(2,1)S(1)}) custom-call(s32[16]{0:T(128)S(1)} %select_reduce_fusion.1.inverse, bf16[256,4096]{1,0:T(8,128)(2,1)S(1)} %copy-done, bf16[512,128]{1,0:T(8,128)(2,1)S(1)} %constant_dynamic-slice_fusion.down, bf16[16,512]{1,0:T(8,128)(2,1)S(1)} %bitcast.61), custom_call_target="tpu_custom_call" | custom-call | tf_op jit(solution)/shard_map/pallas_call | solution.py:196
  58.6 0.0 copy-start.2
  58.6 1.9 %copy-done.2 = bf16[256,8192]{1,0:T(8,128)(2,1)} copy-done((bf16[256,8192]{1,0:T(8,128)(2,1)}, bf16[256,8192]{1,0:T(8,128)(2,1)S(1)}, u32[]{:S(2)}) %copy-start.2) | copy-done | bytes 4194328
  60.5 0.6 gather_fusion
  61.1 0.0 copy-start.4
  61.1 9.4 %fusion = f32[256,2,512]{2,0,1:T(8,128)S(1)} fusion(bf16[8192,2,512]{2,1,0:T(2,128)(2,1)} %param.9, bf16[256,8192]{1,0:T(8,128)(2,1)} %copy-done.2), kind=kOutput, calls=%fused_computation.1 | convolution fusion | flops 4294967296 | bytes 22020096 | tf_op jit(solution)/shard_map/nf,fsc->nsc/dot_general | solution.py:302
  70.6 0.0 copy-start.5
  70.6 0.0 copy-done.4
  70.6 0.0 copy-start.3
  70.6 0.3 fusion.4
  70.9 0.2 reshape_squeeze.3
  71.1 0.1 copy-done.5
  71.2 0.2 reduce-window_2_clone.1
  71.4 0.1 select_reduce_fusion
  71.5 0.5 multiply_cosine_fusion
  72.1 0.5 subtract_convert_fusion
  72.6 0.4 pad_maximum_fusion
  73.0 0.0 copy-done.3
  73.1 0.6 reduce-window.9
  73.7 0.2 slice_reduce_fusion
  73.9 0.1 fusion.15
  74.0 1.4 %convolution_convert_fusion = bf16[512,1024]{1,0:T(8,128)(2,1)} fusion(bf16[256,512]{1,0:T(8,128)(2,1)S(1)} %fusion.8, bf16[256,512]{1,0:T(8,128)(2,1)S(1)} %bitcast.66, s32[256]{0:T(256)S(1)} %multiply_add_fusion), kind=kOutput, calls=%fused_computation.4 | convolution fusion | flops 270139392 | bytes 1573888 | tf_op jit(solution)/shard_map/dot_general | solution.py:314
  75.4 29.0 %shard_map.83 = bf16[16,32,1024]{2,1,0:T(8,128)(2,1)} custom-call(bf16[16,32,1024]{2,1,0:T(8,128)(2,1)} %bitcast.63), custom_call_target="tpu_custom_call" | custom-call | tf_op jit(solution)/shard_map/pallas_call | solution.py:253
  104.4 2.6 %reshape.128 = bf16[512,2,512]{2,1,0:T(2,128)(2,1)} reshape(bf16[16,32,1024]{2,1,0:T(8,128)(2,1)} %shard_map.83) | data formatting | bytes 2097152 | tf_op jit(solution)/shard_map/reshape | solution.py:316
  (14 shorter events, 0.2 us)
Async XLA Ops:
  1.8 1.6 %copy-start = (bf16[256,4096]{1,0:T(8,128)(2,1)S(1)}, bf16[256,4096]{1,0:T(8,128)(2,1)}, u32[]{:S(2)}) copy-start(bf16[256,4096]{1,0:T(8,128)(2,1)} %tokens.1) | copy-start | bytes 6291460
  3.4 0.7 copy-start.1
  58.6 1.9 %copy-start.2 = (bf16[256,8192]{1,0:T(8,128)(2,1)}, bf16[256,8192]{1,0:T(8,128)(2,1)S(1)}, u32[]{:S(2)}) copy-start(bf16[256,8192]{1,0:T(8,128)(2,1)S(1)} %get-tuple-element.8) | copy-start | bytes 12582916
  61.1 9.5 %copy-start.4 = (bf16[2,512]{1,0:T(2,128)(2,1)S(1)}, bf16[2,512]{1,0:T(2,128)(2,1)}, u32[]{:S(2)}) copy-start(bf16[2,512]{1,0:T(2,128)(2,1)} %param.10) | copy-start | bytes 6148
  70.6 0.7 copy-start.5
  70.6 2.5 %copy-start.3 = (s32[256]{0:T(256)S(1)}, s32[256]{0:T(256)}, u32[]{:S(2)}) copy-start(s32[256]{0:T(256)} %param.15) | copy-start | bytes 3076

commit v4 on v3

--- a/solution.py
+++ b/solution.py
@@ -92,6 +92,20 @@
     columns = pl.ds(pl.multiple_of(part * features, features), features)
     chunk_rows = row_count // CHUNKS
     copies = []
+    arriving = []
+    for chunk in range(CHUNKS):
+        for step in range(1, shards):
+            piece = pl.ds(chunk * chunk_rows, chunk_rows)
+            arriving.append(
+                pltpu.make_async_remote_copy(
+                    src_ref=tokens.at[piece],
+                    dst_ref=rows_out.at[piece, columns],
+                    send_sem=token_send.at[step, chunk],
+                    recv_sem=token_recv.at[step, chunk],
+                    device_id={"tensor": (part + step) % shards},
+                )
+            )
+            arriving[-1].start()
     sends = []
     for step in range(1, chips):
         sends.append(
@@ -104,19 +118,6 @@
             )
         )
         sends[-1].start()
-    for chunk in range(CHUNKS):
-        for step in range(1, shards):
-            piece = pl.ds(chunk * chunk_rows, chunk_rows)
-            copies.append(
-                pltpu.make_async_remote_copy(
-                    src_ref=tokens.at[piece],
-                    dst_ref=rows_out.at[piece, columns],
-                    send_sem=token_send.at[step, chunk],
-                    recv_sem=token_recv.at[step, chunk],
-                    device_id={"tensor": (part + step) % shards},
-                )
-            )
-            copies[-1].start()
     copies.append(
         pltpu.make_async_remote_copy(
             src_ref=down,
@@ -165,24 +166,30 @@
     for copy in own:
         copy.wait()
 
-    total = jnp.zeros(low_out.shape[1:], jnp.float32)
-    for owner in range(groups):
-        block = pl.ds(owner * block_rows, block_rows)
-        factor = down_all[inverse[owner]]
-        total += jnp.dot(rows_out[:, block], factor, preferred_element_type=jnp.float32)
-    low_out[part] = (adapter_scale * total).astype(low_out.dtype)
     copies = []
-    for step in range(1, shards):
-        copies.append(
-            pltpu.make_async_remote_copy(
-                src_ref=low_out.at[part],
-                dst_ref=low_out.at[part],
-                send_sem=low_send.at[step],
-                recv_sem=low_recv.at[step],
-                device_id={"tensor": (part + step) % shards},
-            )
-        )
-        copies[-1].start()
+    for chunk in range(CHUNKS):
+        piece = pl.ds(chunk * chunk_rows, chunk_rows)
+        for step in range(1, shards):
+            arriving[chunk * (shards - 1) + step - 1].wait_recv()
+        total = jnp.zeros((chunk_rows, down.shape[1]), jnp.float32)
+        for owner in range(groups):
+            block = pl.ds(owner * block_rows, block_rows)
+            factor = down_all[inverse[owner]]
+            total += jnp.dot(rows_out[piece, block], factor, preferred_element_type=jnp.float32)
+        low_out[part, piece] = (adapter_scale * total).astype(low_out.dtype)
+        for step in range(1, shards):
+            copies.append(
+                pltpu.make_async_remote_copy(
+                    src_ref=low_out.at[part, piece],
+                    dst_ref=low_out.at[part, piece],
+                    send_sem=low_send.at[step, chunk],
+                    recv_sem=low_recv.at[step, chunk],
+                    device_id={"tensor": (part + step) % shards},
+                )
+            )
+            copies[-1].start()
+    for copy in arriving:
+        copy.wait_send()
     for copy in copies:
         copy.wait()
 
@@ -213,8 +220,8 @@
             dma((groups,)),
             dma((chips,)),
             dma((chips,)),
-            dma((shards,)),
-            dma((shards,)),
+            dma((shards, CHUNKS)),
+            dma((shards, CHUNKS)),
         ],
         compiler_params=pltpu.CompilerParams(
             collective_id=0, has_side_effects=True, vmem_limit_bytes=24 * 1024 * 1024

time: 107 us -> 106 us (level)
    pallas_call x1, Pallas kernels: 54.5 us -> 53.2 us  [gather_all(): pl.pallas_call(functools.partial(gather_kernel, groups, shards), out_shap...]
where the time goes in v4:
time: 106 us
  Pallas kernels  82.7 us (78%)
  matrix products  11.1 us (10%)
  local copies, waits for them, and re-layouts  9 us (8%)
  other arithmetic  3.24 us (3%)
    pallas_call x1, Pallas kernels, gather_all(): pl.pallas_call(functools.partial(gather_kernel, groups, shards), out_shap...  53.2 us
    pallas_call x1, Pallas kernels, exchange(): pl.pallas_call(functools.partial(exchange_kernel, groups), out_shape=jax....  29.4 us
    dot_general x1, matrix products, body(): jnp.einsum('nf,fsc->nsc', rows, base_key_value_weight, preferred_element_...  9.43 us
    unnamed x14, local copies, waits for them, and re-layouts  5.35 us
    reshape x1, local copies, waits for them, and re-layouts, body(): return arrived.reshape(slot_count, 2, width)  2.62 us

profile of v4, /device:TPU:15, one launch (start us, length us, event | category | flops | bytes accessed | tf_op | source)
XLA Modules:
  0.0 106.2 jit_solution(17368926196598169491)
XLA Ops:
  0.0 1.0 copy.41
  1.0 0.8 select_reduce_fusion.1.inverse
  1.8 0.0 copy-start
  1.8 1.6 %copy-done = bf16[256,4096]{1,0:T(8,128)(2,1)S(1)} copy-done((bf16[256,4096]{1,0:T(8,128)(2,1)S(1)}, bf16[256,4096]{1,0:T(8,128)(2,1)}, u32[]{:S(2)}) %copy-start) | copy-done | bytes 2097176
  3.4 0.0 copy-start.1
  3.4 0.7 copy-done.1
  4.1 53.2 %shard_map.82 = (bf16[256,8192]{1,0:T(8,128)(2,1)S(1)}, bf16[2,256,128]{2,1,0:T(8,128)(2,1)S(1)}, bf16[16,16,512]{2,1,0:T(8,128)(2,1)S(1)}) custom-call(s32[16]{0:T(128)S(1)} %select_reduce_fusion.1.inverse, bf16[256,4096]{1,0:T(8,128)(2,1)S(1)} %copy-done, bf16[512,128]{1,0:T(8,128)(2,1)S(1)} %constant_dynamic-slice_fusion.down, bf16[16,512]{1,0:T(8,128)(2,1)S(1)} %bitcast.61), custom_call_target="tpu_custom_call" | custom-call | tf_op jit(solution)/shard_map/pallas_call | solution.py:203
  57.3 0.0 copy-start.2
  57.3 1.9 %copy-done.2 = bf16[256,8192]{1,0:T(8,128)(2,1)} copy-done((bf16[256,8192]{1,0:T(8,128)(2,1)}, bf16[256,8192]{1,0:T(8,128)(2,1)S(1)}, u32[]{:S(2)}) %copy-start.2) | copy-done | bytes 4194328
  59.3 0.6 gather_fusion
  59.8 0.0 copy-start.4
  59.8 9.4 %fusion = f32[256,2,512]{2,0,1:T(8,128)S(1)} fusion(bf16[8192,2,512]{2,1,0:T(2,128)(2,1)} %param.9, bf16[256,8192]{1,0:T(8,128)(2,1)} %copy-done.2), kind=kOutput, calls=%fused_computation.1 | convolution fusion | flops 4294967296 | bytes 22020096 | tf_op jit(solution)/shard_map/nf,fsc->nsc/dot_general | solution.py:309
  69.3 0.0 copy-start.5
  69.3 0.0 copy-done.4
  69.3 0.0 copy-start.3
  69.3 0.3 fusion.4
  69.7 0.2 reshape_squeeze.3
  69.9 0.1 copy-done.5
  69.9 0.2 reduce-window_2_clone.1
  70.1 0.1 select_reduce_fusion
  70.2 0.5 multiply_cosine_fusion
  70.8 0.5 subtract_convert_fusion
  71.3 0.4 pad_maximum_fusion
  71.8 0.0 copy-done.3
  71.8 0.6 reduce-window.9
  72.4 0.2 slice_reduce_fusion
  72.6 0.1 fusion.15
  72.7 1.4 %convolution_convert_fusion = bf16[512,1024]{1,0:T(8,128)(2,1)} fusion(bf16[256,512]{1,0:T(8,128)(2,1)S(1)} %fusion.8, bf16[256,512]{1,0:T(8,128)(2,1)S(1)} %bitcast.66, s32[256]{0:T(256)S(1)} %multiply_add_fusion), kind=kOutput, calls=%fused_computation.4 | convolution fusion | flops 270139392 | bytes 1573888 | tf_op jit(solution)/shard_map/dot_general | solution.py:321
  74.1 29.4 %shard_map.83 = bf16[16,32,1024]{2,1,0:T(8,128)(2,1)} custom-call(bf16[16,32,1024]{2,1,0:T(8,128)(2,1)} %bitcast.63), custom_call_target="tpu_custom_call" | custom-call | tf_op jit(solution)/shard_map/pallas_call | solution.py:260
  103.6 2.6 %reshape.128 = bf16[512,2,512]{2,1,0:T(2,128)(2,1)} reshape(bf16[16,32,1024]{2,1,0:T(8,128)(2,1)} %shard_map.83) | data formatting | bytes 2097152 | tf_op jit(solution)/shard_map/reshape | solution.py:323
  (14 shorter events, 0.2 us)
Async XLA Ops:
  1.8 1.6 %copy-start = (bf16[256,4096]{1,0:T(8,128)(2,1)S(1)}, bf16[256,4096]{1,0:T(8,128)(2,1)}, u32[]{:S(2)}) copy-start(bf16[256,4096]{1,0:T(8,128)(2,1)} %tokens.1) | copy-start | bytes 6291460
  3.4 0.7 copy-start.1
  57.3 1.9 %copy-start.2 = (bf16[256,8192]{1,0:T(8,128)(2,1)}, bf16[256,8192]{1,0:T(8,128)(2,1)S(1)}, u32[]{:S(2)}) copy-start(bf16[256,8192]{1,0:T(8,128)(2,1)S(1)} %get-tuple-element.8) | copy-start | bytes 12582916
  59.8 9.5 %copy-start.4 = (bf16[2,512]{1,0:T(2,128)(2,1)S(1)}, bf16[2,512]{1,0:T(2,128)(2,1)}, u32[]{:S(2)}) copy-start(bf16[2,512]{1,0:T(2,128)(2,1)} %param.10) | copy-start | bytes 6148
  69.3 0.7 copy-start.5
  69.3 2.5 %copy-start.3 = (s32[256]{0:T(256)S(1)}, s32[256]{0:T(256)}, u32[]{:S(2)}) copy-start(s32[256]{0:T(256)} %param.15) | copy-start | bytes 3076
